TPU v7x, 512 devices: a whole 4x4x16 slice. The times are simulated.
512 devices in a mesh: seq: 32 (over z, core), head: 16 (over y, x).
Axes of the slice: x: 4, y: 4, z: 16, core: 2. Of those that a mesh axis runs over, the one named last changes fastest.
Arguments:
- query_in: bfloat16 [65536, 2048], P(('seq', 'head')), may hold values from -4.6 to 4.6
- key_in: bfloat16 [65536, 2048], P(('seq', 'head')), may hold values from -4.6 to 4.6
- value_in: bfloat16 [65536, 2048], P(('seq', 'head')), may hold values from -6 to 6
- grad_out: bfloat16 [65536, 2048], P(('seq', 'head')), may hold values from -6 to 6
- module_lengths: int32 [512], replicated, may hold values from 1 to 256, 65536 in all
Outputs:
- attn_out: bfloat16 [65536, 2048], P(('seq', 'head'))
- grad_query: bfloat16 [65536, 2048], P(('seq', 'head'))
- grad_key: bfloat16 [65536, 2048], P(('seq', 'head'))
- grad_value: bfloat16 [65536, 2048], P(('seq', 'head'))
Inputs may be any that keep to these rules, and one draw needn't show every extreme that they name: `module_lengths`: the lengths sum to 65536; the longest is exactly 256.
All inputs are finite; a program needn't handle non-finite values.
Results may differ from a plain program's by a relative error of at most 0.03.
Values may be sent and summed in bfloat16 or wider, within the bound.
A program may use at most 64 MiB of HBM per device.

v0:
```python
import math
import jax
import jax.numpy as jnp
from jax import lax
from jax.sharding import PartitionSpec as P

HEAD_DIM = 128


def shifted(value, axis, by):
    peers = lax.axis_size(axis)
    pairs = [(i, i + by) for i in range(peers) if 0 <= i + by < peers]
    return lax.ppermute(value, axis, pairs)


def module_ids(module_lengths, positions):
    module_ends = jnp.cumsum(module_lengths)
    counted = jnp.sum((positions[:, None] >= module_ends[None, :]).astype(jnp.int32), axis=1)
    return jnp.where(positions >= 0, counted, -1)


def allowed_pairs(module_lengths, query_pos, key_pos):
    same = (
        module_ids(module_lengths, query_pos)[:, None]
        == module_ids(module_lengths, key_pos)[None, :]
    )
    return same & (key_pos[None, :] <= query_pos[:, None])


def score_grads(grad_rows, value_block, weights, row_delta, score_scale):
    dprobs = jnp.einsum("qd,kd->qk", grad_rows, value_block, preferred_element_type=jnp.float32)
    return (weights * (dprobs - row_delta[:, None]) * score_scale).astype(jnp.bfloat16)


def key_terms(dscores, weight_bf, query_rows, grad_rows):
    key_grad = jnp.einsum("qk,qd->kd", dscores, query_rows, preferred_element_type=jnp.float32)
    value_grad = jnp.einsum("qk,qd->kd", weight_bf, grad_rows, preferred_element_type=jnp.float32)
    return (key_grad, value_grad)


def one_block(query_rows, key_block, value_block, grad_rows, allowed, score_scale):
    scores = (
        jnp.einsum("qd,kd->qk", query_rows, key_block, preferred_element_type=jnp.float32)
        * score_scale
    )
    row_top = jnp.max(jnp.where(allowed, scores, -jnp.inf), axis=1, keepdims=True)
    row_total = jnp.sum(jnp.where(allowed, jnp.exp(scores - row_top), 0.0), axis=1, keepdims=True)
    log_total = row_top + jnp.log(row_total)
    weights = jnp.where(allowed, jnp.exp(scores - log_total), 0.0)
    weight_bf = weights.astype(jnp.bfloat16)
    attn_rows = jnp.einsum(
        "qk,kd->qd", weight_bf, value_block, preferred_element_type=jnp.float32
    ).astype(jnp.bfloat16)
    row_delta = jnp.sum(grad_rows.astype(jnp.float32) * attn_rows.astype(jnp.float32), axis=1)
    dscores = score_grads(grad_rows, value_block, weights, row_delta, score_scale)
    grad_q = jnp.einsum("qk,kd->qd", dscores, key_block, preferred_element_type=jnp.float32).astype(
        jnp.bfloat16
    )
    key_grad, value_grad = key_terms(dscores, weight_bf, query_rows, grad_rows)
    return (attn_rows, grad_q, key_grad, value_grad, log_total[:, 0], row_delta)


def shards(query_in, key_in, value_in, grad_out, module_lengths):
    head_q, head_k, head_v, head_do = (
        lax.all_to_all(query_in, "head", split_axis=1, concat_axis=0, tiled=True),
        lax.all_to_all(key_in, "head", split_axis=1, concat_axis=0, tiled=True),
        lax.all_to_all(value_in, "head", split_axis=1, concat_axis=0, tiled=True),
        lax.all_to_all(grad_out, "head", split_axis=1, concat_axis=0, tiled=True),
    )
    row_count = head_q.shape[0]
    width = head_q.shape[1]
    local_heads = width // HEAD_DIM
    prior_rows = row_count // 8
    score_scale = HEAD_DIM ** (-0.5)
    tail_start = row_count - prior_rows
    prior_k, prior_v = shifted((head_k[tail_start:], head_v[tail_start:]), "seq", 1)
    row_start = lax.axis_index("seq") * row_count
    query_pos = row_start + jnp.arange(row_count, dtype=jnp.int32)
    before_pos = row_start - prior_rows + jnp.arange(prior_rows, dtype=jnp.int32)
    key_pos = jnp.concatenate([before_pos, query_pos])
    block_rows = math.gcd(row_count, 512)
    block_count = row_count // block_rows
    pos_blocks = query_pos.reshape(block_count, block_rows)

    def by_head(flat, rows):
        return jnp.moveaxis(flat.reshape(rows, local_heads, HEAD_DIM), 1, 0)

    def to_flat(stacked):
        return jnp.moveaxis(stacked, 0, 1).reshape(stacked.shape[1], width)

    query_h = by_head(head_q, row_count)
    grad_h = by_head(head_do, row_count)
    key_h = by_head(jnp.concatenate([prior_k, head_k], axis=0), row_count + prior_rows)
    value_h = by_head(jnp.concatenate([prior_v, head_v], axis=0), row_count + prior_rows)

    def run_head(packed):
        query_rows, key_block, value_block, grad_rows = packed
        query_blocks = query_rows.reshape(block_count, block_rows, HEAD_DIM)
        grad_blocks = grad_rows.reshape(block_count, block_rows, HEAD_DIM)

        def run_block(inner):
            query_part, grad_part, pos_part = inner
            allowed = allowed_pairs(module_lengths, pos_part, key_pos)
            return one_block(query_part, key_block, value_block, grad_part, allowed, score_scale)

        attn_b, grad_qb, key_b, value_b, lse_b, delta_b = lax.map(
            run_block, (query_blocks, grad_blocks, pos_blocks)
        )
        return (
            attn_b.reshape(row_count, HEAD_DIM),
            grad_qb.reshape(row_count, HEAD_DIM),
            jnp.sum(key_b, axis=0),
            jnp.sum(value_b, axis=0),
            lse_b.reshape(row_count),
            delta_b.reshape(row_count),
        )

    attn_h, grad_qh, key_grad, value_grad, log_total, row_delta = lax.map(
        run_head, (query_h, key_h, value_h, grad_h)
    )
    attn_flat = to_flat(attn_h)
    attn_back = lax.all_to_all(attn_flat, "head", split_axis=0, concat_axis=1, tiled=True)
    grad_q = to_flat(grad_qh)
    later_k, later_v = shifted((key_grad[:, :prior_rows], value_grad[:, :prior_rows]), "seq", -1)
    key_total = key_grad[:, prior_rows:].at[:, tail_start:].add(later_k)
    value_total = value_grad[:, prior_rows:].at[:, tail_start:].add(later_v)
    grad_k = to_flat(key_total.astype(jnp.bfloat16))
    grad_v = to_flat(value_total.astype(jnp.bfloat16))
    back_q, back_k, back_v = (
        lax.all_to_all(grad_q, "head", split_axis=0, concat_axis=1, tiled=True),
        lax.all_to_all(grad_k, "head", split_axis=0, concat_axis=1, tiled=True),
        lax.all_to_all(grad_v, "head", split_axis=0, concat_axis=1, tiled=True),
    )
    return (attn_back, back_q, back_k, back_v)


def solution(mesh):
    placed = (
        P(("seq", "head"), None),
        P(("seq", "head"), None),
        P(("seq", "head"), None),
        P(("seq", "head"), None),
        P(),
    )
    return jax.shard_map(
        shards,
        mesh=mesh,
        in_specs=placed,
        out_specs=(
            P(("seq", "head"), None),
            P(("seq", "head"), None),
            P(("seq", "head"), None),
            P(("seq", "head"), None),
        ),
        check_vma=False,
    )
```

profile of v0, /device:TPU:225, one launch (start us, length us, event | category | flops | bytes accessed | tf_op | source)
XLA Modules:
  0.0 204.6 jit_solution(12996659685108868162)
XLA Ops:
  2.6 6.8 %all-to-all-start.1 = ((bf16[128,16,128]{2,0,1:T(8,128)(2,1)}), bf16[128,16,128]{2,0,1:T(8,128)(2,1)S(1)}, u32[]{:S(2)}, u32[]{:S(2)}) async-start(bf16[128,16,128]{2,0,1:T(8,128)(2,1)} %copy_bitcast_fusion.1), calls=%async_computation.1 | async-start | bytes 1048576 | tf_op jit(solution)/shard_map/all_to_all | solution.py:66
  11.3 8.5 %all-to-all-done.1 = bf16[128,16,128]{2,0,1:T(8,128)(2,1)S(1)} async-done(((bf16[128,16,128]{2,0,1:T(8,128)(2,1)}), bf16[128,16,128]{2,0,1:T(8,128)(2,1)S(1)}, u32[]{:S(2)}, u32[]{:S(2)}) %all-to-all-start.1) | async-done | bytes 524320 | tf_op jit(solution)/shard_map/all_to_all | solution.py:66
  19.9 3.6 %all-to-all-start.2 = ((bf16[128,16,128]{2,0,1:T(8,128)(2,1)}), bf16[128,16,128]{2,0,1:T(8,128)(2,1)S(1)}, u32[]{:S(2)}, u32[]{:S(2)}) async-start(bf16[128,16,128]{2,0,1:T(8,128)(2,1)} %copy_bitcast_fusion), calls=%async_computation.2 | async-start | bytes 1048576 | tf_op jit(solution)/shard_map/all_to_all | solution.py:67
  25.5 7.6 %all-to-all-done.2 = bf16[128,16,128]{2,0,1:T(8,128)(2,1)S(1)} async-done(((bf16[128,16,128]{2,0,1:T(8,128)(2,1)}), bf16[128,16,128]{2,0,1:T(8,128)(2,1)S(1)}, u32[]{:S(2)}, u32[]{:S(2)}) %all-to-all-start.2) | async-done | bytes 524320 | tf_op jit(solution)/shard_map/all_to_all | solution.py:67
  33.1 3.6 %all-to-all-start.3 = ((bf16[128,16,128]{0,2,1:T(8,128)(2,1)}), bf16[128,16,128]{0,2,1:T(8,128)(2,1)S(1)}, u32[]{:S(2)}, u32[]{:S(2)}) async-start(bf16[128,16,128]{0,2,1:T(8,128)(2,1)} %bitcast.18), calls=%async_computation.3 | async-start | bytes 1048576 | tf_op jit(solution)/shard_map/all_to_all | solution.py:68
  38.2 7.5 %collective-permute-start = (bf16[256,128]{1,0:T(8,128)(2,1)S(1)}, bf16[256,128]{1,0:T(8,128)(2,1)S(1)}, u32[]{:S(2)}, u32[]{:S(2)}) collective-permute-start(bf16[256,128]{1,0:T(8,128)(2,1)S(1)} %bitcast.152), channel_id=1, source_target_pairs={{0,16},{16,32},{32,48},{48,64},{64,80},{80,96},{96,112},{112,128},... | collective-permute-start | bytes 196616 | tf_op jit(solution)/shard_map/ppermute | solution.py:13
  47.7 6.9 %all-to-all-start = ((bf16[128,16,128]{2,0,1:T(8,128)(2,1)}), bf16[128,16,128]{2,0,1:T(8,128)(2,1)S(1)}, u32[]{:S(2)}, u32[]{:S(2)}) async-start(bf16[128,16,128]{2,0,1:T(8,128)(2,1)} %copy_bitcast_fusion.2), calls=%async_computation | async-start | bytes 1048576 | tf_op jit(solution)/shard_map/all_to_all | solution.py:65
  55.8 9.4 %all-to-all-done = bf16[128,16,128]{2,0,1:T(8,128)(2,1)S(1)} async-done(((bf16[128,16,128]{2,0,1:T(8,128)(2,1)}), bf16[128,16,128]{2,0,1:T(8,128)(2,1)S(1)}, u32[]{:S(2)}, u32[]{:S(2)}) %all-to-all-start) | async-done | bytes 524320 | tf_op jit(solution)/shard_map/all_to_all | solution.py:65
  65.1 74.4 %while.33 = (s32[]{:T(128)}, bf16[4,512,128]{2,1,0:T(8,128)(2,1)}, bf16[4,512,128]{2,1,0:T(8,128)(2,1)}, f32[4,2304,128]{2,1,0:T(8,128)}, f32[4,2304,128]{2,1,0:...) while((s32[]{:T(128)}, bf16[4,512,128]{2,1,0:T(8,128)(2,1)}, ...), condition=%wide.region_8.9_spmd, body=%wide.region_2.8_spmd.sunk | while | flops 1855588608 | bytes 72957736 | solution.py:106
  70.5 2.7 %fusion.56 = f32[4,2304,128]{2,1,0:T(8,128)} fusion(f32[4,2304,128]{2,1,0:T(8,128)} %get-tuple-element.443, s32[]{:T(128)} %get-tuple-element.439, bf16[1,512,128]{2,1,0:T(8,128)(2,1)S(1)} %constant_dynamic-slice_fusion.4, f32[512,2304]{1,0:T(8,128)S(1)} %get-tuple-element.421, f32[512]{0:T(512)S(1)} %log_add_fusion.2, ...), kind=kOutput, calls=%fused_computation.11.clone.1 | convolution fusion | flops 309067776 | bytes 6054400 | tf_op jit(solution)/shard_map/while/body/eval_jaxpr/while/body/eval_jaxpr/qk,qd->kd/dot_general | solution.py:37
  73.4 3.9 %multiply_reduce_fusion.2 = (f32[512]{0:T(512)S(1)}, bf16[512,128]{0,1:T(8,128)(2,1)S(1)}) fusion(bf16[1,512,128]{1,2,0:T(8,128)(2,1)S(1)} %copy.99, bf16[2304,128]{1,0:T(8,128)(2,1)S(1)} %copy-done.2, f32[512,2304]{1,0:T(8,128)} %copy-done.1, f32[512]{0:T(512)S(1)} %log_add_fusion.2, s32[512]{0:T(512)S(1)} %bitcast.148, ...), kind=kOutput, calls=%fused_computation.20.clone.1 | convolution fusion | flops 309394944 | bytes 5597184 | tf_op jit(solution)/shard_map/while/body/eval_jaxpr/while/body/eval_jaxpr/qk,kd->qd/dot_general | solution.py:51
  92.0 3.9 %multiply_reduce_fusion.2 = (f32[512]{0:T(512)S(1)}, bf16[512,128]{0,1:T(8,128)(2,1)S(1)}) fusion(bf16[1,512,128]{1,2,0:T(8,128)(2,1)S(1)} %copy.99, bf16[2304,128]{1,0:T(8,128)(2,1)S(1)} %copy-done.2, f32[512,2304]{1,0:T(8,128)} %copy-done.1, f32[512]{0:T(512)S(1)} %log_add_fusion.2, s32[512]{0:T(512)S(1)} %bitcast.148, ...), kind=kOutput, calls=%fused_computation.20.clone.1 | convolution fusion | flops 309394944 | bytes 5597184 | tf_op jit(solution)/shard_map/while/body/eval_jaxpr/while/body/eval_jaxpr/qk,kd->qd/dot_general | solution.py:51
  110.6 3.9 %multiply_reduce_fusion.2 = (f32[512]{0:T(512)S(1)}, bf16[512,128]{0,1:T(8,128)(2,1)S(1)}) fusion(bf16[1,512,128]{1,2,0:T(8,128)(2,1)S(1)} %copy.99, bf16[2304,128]{1,0:T(8,128)(2,1)S(1)} %copy-done.2, f32[512,2304]{1,0:T(8,128)} %copy-done.1, f32[512]{0:T(512)S(1)} %log_add_fusion.2, s32[512]{0:T(512)S(1)} %bitcast.148, ...), kind=kOutput, calls=%fused_computation.20.clone.1 | convolution fusion | flops 309394944 | bytes 5597184 | tf_op jit(solution)/shard_map/while/body/eval_jaxpr/while/body/eval_jaxpr/qk,kd->qd/dot_general | solution.py:51
  126.3 2.8 %fusion.56 = f32[4,2304,128]{2,1,0:T(8,128)} fusion(f32[4,2304,128]{2,1,0:T(8,128)} %get-tuple-element.443, s32[]{:T(128)} %get-tuple-element.439, bf16[1,512,128]{2,1,0:T(8,128)(2,1)S(1)} %constant_dynamic-slice_fusion.4, f32[512,2304]{1,0:T(8,128)S(1)} %get-tuple-element.421, f32[512]{0:T(512)S(1)} %log_add_fusion.2, ...), kind=kOutput, calls=%fused_computation.11.clone.1 | convolution fusion | flops 309067776 | bytes 6054400 | tf_op jit(solution)/shard_map/while/body/eval_jaxpr/while/body/eval_jaxpr/qk,qd->kd/dot_general | solution.py:37
  129.2 3.9 %multiply_reduce_fusion.2 = (f32[512]{0:T(512)S(1)}, bf16[512,128]{0,1:T(8,128)(2,1)S(1)}) fusion(bf16[1,512,128]{1,2,0:T(8,128)(2,1)S(1)} %copy.99, bf16[2304,128]{1,0:T(8,128)(2,1)S(1)} %copy-done.2, f32[512,2304]{1,0:T(8,128)} %copy-done.1, f32[512]{0:T(512)S(1)} %log_add_fusion.2, s32[512]{0:T(512)S(1)} %bitcast.148, ...), kind=kOutput, calls=%fused_computation.20.clone.1 | convolution fusion | flops 309394944 | bytes 5597184 | tf_op jit(solution)/shard_map/while/body/eval_jaxpr/while/body/eval_jaxpr/qk,kd->qd/dot_general | solution.py:51
  139.6 13.3 %all_to_all.146 = bf16[16,128,128]{2,1,0:T(8,128)(2,1)S(1)} all-to-all(bf16[16,128,128]{2,1,0:T(8,128)(2,1)} %bitcast.150), channel_id=1, replica_groups=mesh['seq'=32,'head'=16] {'head'}, dimensions={0} | all-to-all | bytes 1048576 | tf_op jit(solution)/shard_map/all_to_all | solution.py:122
  152.9 3.6 %all-to-all-start.5 = ((bf16[16,128,128]{2,1,0:T(8,128)(2,1)}), bf16[16,128,128]{2,1,0:T(8,128)(2,1)S(1)}, u32[]{:S(2)}, u32[]{:S(2)}) async-start(bf16[16,128,128]{2,1,0:T(8,128)(2,1)} %bitcast.151), calls=%async_computation.5 | async-start | bytes 1048576 | tf_op jit(solution)/shard_map/all_to_all | solution.py:130
  156.5 2.7 %reduce_sum.65 = f32[2304,128]{1,0:T(8,128)S(1)} reduce(f32[4,2304,128]{2,1,0:T(8,128)} %get-tuple-element.213, f32[]{:T(128)} %constant.129.clone.1), dimensions={0}, to_apply=%region_10.11 | reduce | flops 884736 | bytes 5898244 | tf_op jit(solution)/shard_map/while/body/eval_jaxpr/reduce_sum | solution.py:113
  159.2 4.6 %collective-permute-start.3 = (f32[1,256,128]{2,1,0:T(8,128)S(1)}, f32[1,256,128]{2,1,0:T(8,128)S(1)}, u32[]{:S(2)}, u32[]{:S(2)}) collective-permute-start(f32[1,256,128]{2,1,0:T(8,128)S(1)} %slice.103), channel_id=1, source_target_pairs={{16,0},{32,16},{48,32},{64,48},{80,64},{96,80},{112,96},{128,112},... | collective-permute-start | bytes 393224 | tf_op jit(solution)/shard_map/ppermute | solution.py:13
  168.1 6.6 %all-to-all-start.7 = ((bf16[16,128,128]{2,1,0:T(8,128)(2,1)}), bf16[16,128,128]{2,1,0:T(8,128)(2,1)S(1)}, u32[]{:S(2)}, u32[]{:S(2)}) async-start(bf16[16,128,128]{2,1,0:T(8,128)(2,1)} %bitcast.32), calls=%async_computation.7 | async-start | bytes 1048576 | tf_op jit(solution)/shard_map/all_to_all | solution.py:132
  174.6 2.7 %reduce_sum.64 = f32[2304,128]{1,0:T(8,128)S(1)} reduce(f32[4,2304,128]{2,1,0:T(8,128)} %get-tuple-element.212, f32[]{:T(128)} %constant.129.clone.1), dimensions={0}, to_apply=%region_9.10 | reduce | flops 884736 | bytes 5898244 | tf_op jit(solution)/shard_map/while/body/eval_jaxpr/reduce_sum | solution.py:112
  180.2 4.7 %collective-permute-done.2 = f32[1,256,128]{2,1,0:T(8,128)S(1)} collective-permute-done((f32[1,256,128]{2,1,0:T(8,128)S(1)}, f32[1,256,128]{2,1,0:T(8,128)S(1)}, u32[]{:S(2)}, u32[]{:S(2)}) %collective-permute-start.2) | collective-permute-done | bytes 131104 | tf_op jit(solution)/shard_map/ppermute | solution.py:13
  187.1 5.1 %all-to-all-start.6 = ((bf16[16,128,128]{2,1,0:T(8,128)(2,1)}), bf16[16,128,128]{2,1,0:T(8,128)(2,1)S(1)}, u32[]{:S(2)}, u32[]{:S(2)}) async-start(bf16[16,128,128]{2,1,0:T(8,128)(2,1)} %bitcast.28), calls=%async_computation.6 | async-start | bytes 1048576 | tf_op jit(solution)/shard_map/all_to_all | solution.py:131
  196.1 7.2 %all-to-all-done.6 = bf16[16,128,128]{2,1,0:T(8,128)(2,1)S(1)} async-done(((bf16[16,128,128]{2,1,0:T(8,128)(2,1)}), bf16[16,128,128]{2,1,0:T(8,128)(2,1)S(1)}, u32[]{:S(2)}, u32[]{:S(2)}) %all-to-all-start.6) | async-done | bytes 524320 | tf_op jit(solution)/shard_map/all_to_all | solution.py:131
  (155 shorter events, 77.8 us)
Async XLA Ops:
  0.6 36.1 %copy-start.4 = (s32[512]{0:T(512)S(1)}, s32[512]{0:T(512)}, u32[]{:S(2)}) copy-start(s32[512]{0:T(512)} %param.15) | copy-start | bytes 6148
  1.7 35.6 %copy-start.3 = (bf16[128,2048]{1,0:T(8,128)(2,1)S(1)}, bf16[128,2048]{1,0:T(8,128)(2,1)}, u32[]{:S(2)}) copy-start(bf16[128,2048]{1,0:T(8,128)(2,1)} %param.11) | copy-start | bytes 1572868
  2.6 17.3 %all-to-all-start.1 = ((bf16[128,16,128]{2,0,1:T(8,128)(2,1)}), bf16[128,16,128]{2,0,1:T(8,128)(2,1)S(1)}, u32[]{:S(2)}, u32[]{:S(2)}) async-start(bf16[128,16,128]{2,0,1:T(8,128)(2,1)} %copy_bitcast_fusion.1), calls=%async_computation.1 | async-start | bytes 1048576 | tf_op jit(solution)/shard_map/all_to_all | solution.py:66
  19.9 13.2 %all-to-all-start.2 = ((bf16[128,16,128]{2,0,1:T(8,128)(2,1)}), bf16[128,16,128]{2,0,1:T(8,128)(2,1)S(1)}, u32[]{:S(2)}, u32[]{:S(2)}) async-start(bf16[128,16,128]{2,0,1:T(8,128)(2,1)} %copy_bitcast_fusion), calls=%async_computation.2 | async-start | bytes 1048576 | tf_op jit(solution)/shard_map/all_to_all | solution.py:67
  33.1 14.5 %all-to-all-start.3 = ((bf16[128,16,128]{0,2,1:T(8,128)(2,1)}), bf16[128,16,128]{0,2,1:T(8,128)(2,1)S(1)}, u32[]{:S(2)}, u32[]{:S(2)}) async-start(bf16[128,16,128]{0,2,1:T(8,128)(2,1)} %bitcast.18), calls=%async_computation.3 | async-start | bytes 1048576 | tf_op jit(solution)/shard_map/all_to_all | solution.py:68
  38.2 16.6 %collective-permute-start = (bf16[256,128]{1,0:T(8,128)(2,1)S(1)}, bf16[256,128]{1,0:T(8,128)(2,1)S(1)}, u32[]{:S(2)}, u32[]{:S(2)}) collective-permute-start(bf16[256,128]{1,0:T(8,128)(2,1)S(1)} %bitcast.152), channel_id=1, source_target_pairs={{0,16},{16,32},{32,48},{48,64},{64,80},{80,96},{96,112},{112,128},... | collective-permute-start | bytes 196616 | tf_op jit(solution)/shard_map/ppermute | solution.py:13
  45.7 9.2 %collective-permute-start.1 = (bf16[256,128]{1,0:T(8,128)(2,1)S(1)}, bf16[256,128]{1,0:T(8,128)(2,1)S(1)}, u32[]{:S(2)}, u32[]{:S(2)}) collective-permute-start(bf16[256,128]{1,0:T(8,128)(2,1)S(1)} %bitcast.153), channel_id=1, source_target_pairs={{0,16},{16,32},{32,48},{48,64},{64,80},{80,96},{96,112},{112,128},... | collective-permute-start | bytes 196616 | tf_op jit(solution)/shard_map/ppermute | solution.py:13
  47.7 17.5 %all-to-all-start = ((bf16[128,16,128]{2,0,1:T(8,128)(2,1)}), bf16[128,16,128]{2,0,1:T(8,128)(2,1)S(1)}, u32[]{:S(2)}, u32[]{:S(2)}) async-start(bf16[128,16,128]{2,0,1:T(8,128)(2,1)} %copy_bitcast_fusion.2), calls=%async_computation | async-start | bytes 1048576 | tf_op jit(solution)/shard_map/all_to_all | solution.py:65
  70.5 2.9 %copy-start.2 = (bf16[2304,128]{1,0:T(8,128)(2,1)S(1)}, bf16[2304,128]{1,0:T(8,128)(2,1)}, u32[]{:S(2)}) copy-start(bf16[2304,128]{1,0:T(8,128)(2,1)} %get-tuple-element.464) | copy-start | bytes 1769476 | tf_op jit(solution)/shard_map/while/body/eval_jaxpr/while
  73.4 4.0 %slice-start = ((s8[4718592]{0:T(1024)(128)(4,1)}), s8[4194304]{0:T(1024)(128)(4,1)S(1)}, s32[]{:S(2)}) async-start(s8[4718592]{0:T(1024)(128)(4,1)} %bitcast.120), calls=%async_computation.8 | async-start | bytes 8388608 | tf_op jit(solution)/shard_map/while/body/eval_jaxpr/while
  73.4 3.9 %slice-start.1 = ((s8[4718592]{0:T(1024)(128)(4,1)}), s8[524288]{0:T(1024)(128)(4,1)S(1)}, s32[]{:S(2)}) async-start(s8[4718592]{0:T(1024)(128)(4,1)} %bitcast.120), calls=%async_computation.9 | async-start | bytes 1048576 | tf_op jit(solution)/shard_map/while/body/eval_jaxpr/while
  89.1 2.8 %copy-start.2 = (bf16[2304,128]{1,0:T(8,128)(2,1)S(1)}, bf16[2304,128]{1,0:T(8,128)(2,1)}, u32[]{:S(2)}) copy-start(bf16[2304,128]{1,0:T(8,128)(2,1)} %get-tuple-element.464) | copy-start | bytes 1769476 | tf_op jit(solution)/shard_map/while/body/eval_jaxpr/while
  91.9 4.0 %slice-start = ((s8[4718592]{0:T(1024)(128)(4,1)}), s8[4194304]{0:T(1024)(128)(4,1)S(1)}, s32[]{:S(2)}) async-start(s8[4718592]{0:T(1024)(128)(4,1)} %bitcast.120), calls=%async_computation.8 | async-start | bytes 8388608 | tf_op jit(solution)/shard_map/while/body/eval_jaxpr/while
  92.0 3.9 %slice-start.1 = ((s8[4718592]{0:T(1024)(128)(4,1)}), s8[524288]{0:T(1024)(128)(4,1)S(1)}, s32[]{:S(2)}) async-start(s8[4718592]{0:T(1024)(128)(4,1)} %bitcast.120), calls=%async_computation.9 | async-start | bytes 1048576 | tf_op jit(solution)/shard_map/while/body/eval_jaxpr/while
  110.5 4.0 %slice-start = ((s8[4718592]{0:T(1024)(128)(4,1)}), s8[4194304]{0:T(1024)(128)(4,1)S(1)}, s32[]{:S(2)}) async-start(s8[4718592]{0:T(1024)(128)(4,1)} %bitcast.120), calls=%async_computation.8 | async-start | bytes 8388608 | tf_op jit(solution)/shard_map/while/body/eval_jaxpr/while
  110.6 3.9 %slice-start.1 = ((s8[4718592]{0:T(1024)(128)(4,1)}), s8[524288]{0:T(1024)(128)(4,1)S(1)}, s32[]{:S(2)}) async-start(s8[4718592]{0:T(1024)(128)(4,1)} %bitcast.120), calls=%async_computation.9 | async-start | bytes 1048576 | tf_op jit(solution)/shard_map/while/body/eval_jaxpr/while
  126.3 2.9 %copy-start.2 = (bf16[2304,128]{1,0:T(8,128)(2,1)S(1)}, bf16[2304,128]{1,0:T(8,128)(2,1)}, u32[]{:S(2)}) copy-start(bf16[2304,128]{1,0:T(8,128)(2,1)} %get-tuple-element.464) | copy-start | bytes 1769476 | tf_op jit(solution)/shard_map/while/body/eval_jaxpr/while
  129.2 4.0 %slice-start = ((s8[4718592]{0:T(1024)(128)(4,1)}), s8[4194304]{0:T(1024)(128)(4,1)S(1)}, s32[]{:S(2)}) async-start(s8[4718592]{0:T(1024)(128)(4,1)} %bitcast.120), calls=%async_computation.8 | async-start | bytes 8388608 | tf_op jit(solution)/shard_map/while/body/eval_jaxpr/while
  129.2 3.9 %slice-start.1 = ((s8[4718592]{0:T(1024)(128)(4,1)}), s8[524288]{0:T(1024)(128)(4,1)S(1)}, s32[]{:S(2)}) async-start(s8[4718592]{0:T(1024)(128)(4,1)} %bitcast.120), calls=%async_computation.9 | async-start | bytes 1048576 | tf_op jit(solution)/shard_map/while/body/eval_jaxpr/while
  152.9 15.2 %all-to-all-start.5 = ((bf16[16,128,128]{2,1,0:T(8,128)(2,1)}), bf16[16,128,128]{2,1,0:T(8,128)(2,1)S(1)}, u32[]{:S(2)}, u32[]{:S(2)}) async-start(bf16[16,128,128]{2,1,0:T(8,128)(2,1)} %bitcast.151), calls=%async_computation.5 | async-start | bytes 1048576 | tf_op jit(solution)/shard_map/all_to_all | solution.py:130
  159.2 8.2 %collective-permute-start.3 = (f32[1,256,128]{2,1,0:T(8,128)S(1)}, f32[1,256,128]{2,1,0:T(8,128)S(1)}, u32[]{:S(2)}, u32[]{:S(2)}) collective-permute-start(f32[1,256,128]{2,1,0:T(8,128)S(1)} %slice.103), channel_id=1, source_target_pairs={{16,0},{32,16},{48,32},{64,48},{80,64},{96,80},{112,96},{128,112},... | collective-permute-start | bytes 393224 | tf_op jit(solution)/shard_map/ppermute | solution.py:13
  168.1 19.1 %all-to-all-start.7 = ((bf16[16,128,128]{2,1,0:T(8,128)(2,1)}), bf16[16,128,128]{2,1,0:T(8,128)(2,1)S(1)}, u32[]{:S(2)}, u32[]{:S(2)}) async-start(bf16[16,128,128]{2,1,0:T(8,128)(2,1)} %bitcast.32), calls=%async_computation.7 | async-start | bytes 1048576 | tf_op jit(solution)/shard_map/all_to_all | solution.py:132
  177.4 7.5 %collective-permute-start.2 = (f32[1,256,128]{2,1,0:T(8,128)S(1)}, f32[1,256,128]{2,1,0:T(8,128)S(1)}, u32[]{:S(2)}, u32[]{:S(2)}) collective-permute-start(f32[1,256,128]{2,1,0:T(8,128)S(1)} %slice.100), channel_id=1, source_target_pairs={{16,0},{32,16},{48,32},{64,48},{80,64},{96,80},{112,96},{128,112},... | collective-permute-start | bytes 393224 | tf_op jit(solution)/shard_map/ppermute | solution.py:13
  187.1 16.2 %all-to-all-start.6 = ((bf16[16,128,128]{2,1,0:T(8,128)(2,1)}), bf16[16,128,128]{2,1,0:T(8,128)(2,1)S(1)}, u32[]{:S(2)}, u32[]{:S(2)}) async-start(bf16[16,128,128]{2,1,0:T(8,128)(2,1)} %bitcast.28), calls=%async_computation.6 | async-start | bytes 1048576 | tf_op jit(solution)/shard_map/all_to_all | solution.py:131
  (6 other events, 12.9 us)
where the time goes:
time: 206 us; the launch traced here: 205 us
  matrix products  53.9 us (26%)
  starting transfers between devices  52 us (25%)
  waiting for transfers between devices  41.8 us (20%)
  other arithmetic  22.4 us (11%)
  local copies, waits for them, and re-layouts  19.9 us (10%)
  blocking collectives  13.3 us (6%)
    ppermute x4, starting transfers between devices, shifted(): return lax.ppermute(value, axis, pairs)  16 us
    dot_general x4, matrix products, one_block(): jnp.einsum('qk,kd->qd', weight_bf, value_block, preferred_element_type=jn...  15.7 us
    all_to_all x1, blocking collectives, shards(): lax.all_to_all(attn_flat, 'head', split_axis=0, concat_axis=1, tiled=True)  13.3 us
    dot_general x4, matrix products, key_terms(): jnp.einsum('qk,qd->kd', weight_bf, grad_rows, preferred_element_type=jnp....  10.9 us
    all_to_all x1, waiting for transfers between devices, shards(): lax.all_to_all(query_in, 'head', split_axis=1, concat_axis=0, tiled=True)  9.36 us
    dot_general x4, matrix products, score_grads(): jnp.einsum('qd,kd->qk', grad_rows, value_block, preferred_element_type=jn...  9.12 us
    all_to_all x1, waiting for transfers between devices, shards(): lax.all_to_all(key_in, 'head', split_axis=1, concat_axis=0, tiled=True)  8.54 us
    all_to_all x1, waiting for transfers between devices, shards(): lax.all_to_all(value_in, 'head', split_axis=1, concat_axis=0, tiled=True)  7.61 us
  transfers between devices with their start and end apart: 11, of which 7 were waited for; matrix products, arithmetic and copies ran while one was open for 9% of the time, Pallas kernels for 0%

commit v1 on v0

--- a/solution.py
+++ b/solution.py
@@ -128,7 +128,12 @@
     grad_v = to_flat(value_total.astype(jnp.bfloat16))
     back_q, back_k, back_v = (
         lax.all_to_all(grad_q, "head", split_axis=0, concat_axis=1, tiled=True),
-        lax.all_to_all(grad_k, "head", split_axis=0, concat_axis=1, tiled=True),
+        jnp.concatenate(
+            lax.all_to_all(
+                jnp.stack(jnp.split(grad_k, lax.axis_size("head"), axis=0)), "head", 0, 0
+            ),
+            axis=1,
+        ),
         lax.all_to_all(grad_v, "head", split_axis=0, concat_axis=1, tiled=True),
     )
     return (attn_back, back_q, back_k, back_v)

time: 206 us -> 216 us (1.049)
  blocking collectives: 13.3 us -> 0 us
  local copies, waits for them, and re-layouts: 19.9 us -> 29 us
  waiting for transfers between devices: 41.8 us -> 47.9 us
  matrix products: 53.9 us -> 58.4 us
  starting transfers between devices: 52 us -> 55.1 us
    all_to_all x1 -> x0, blocking collectives: 13.3 us -> none  [shards(): lax.all_to_all(attn_flat, 'head', split_axis=0, concat_axis=1, tiled=True)]
    unnamed x11 -> x26, local copies, waits for them, and re-layouts: 7.13 us -> 16.4 us
    all_to_all x1, waiting for transfers between devices: 0.01 us -> 8.45 us  [shards(): lax.all_to_all(grad_q, 'head', split_axis=0, concat_axis=1, tiled=True)]
    all_to_all x1, waiting for transfers between devices: 1.6 us -> 8.36 us  [shards(): lax.all_to_all(grad_v, 'head', split_axis=0, concat_axis=1, tiled=True)]
    ppermute x4, waiting for transfers between devices: 7.43 us -> 3.07 us  [shifted(): return lax.ppermute(value, axis, pairs)]
    dot_general x4, matrix products: 5.07 us -> 9.35 us  [one_block(): jnp.einsum('qd,kd->qk', query_rows, key_block, preferred_element_type=jnp...]
    all_to_all x1 -> x2, waiting for transfers between devices: 7.24 us -> 3.3 us  [the longest x1 3.29 us: shards(): lax.all_to_all(attn_flat, 'head', split_axis=0, concat_axis=1, tiled=True)]
    all_to_all x1 -> x2, starting transfers between devices: 5.06 us -> 7.16 us  [the longest x1 3.59 us: shards(): lax.all_to_all(attn_flat, 'head', split_axis=0, concat_axis=1, tiled=True)]
  transfers between devices with their start and end apart: 11 -> 12, of which waited for: 7 -> 7; matrix products, arithmetic and copies ran while one was open for 9% -> 12% of each run, Pallas kernels for 0% -> 0%
where the time goes in v1:
time: 216 us; the launch traced here: 214 us
  matrix products  58.4 us (27%)
  starting transfers between devices  55.1 us (26%)
  waiting for transfers between devices  47.9 us (22%)
  local copies, waits for them, and re-layouts  29 us (13%)
  other arithmetic  22.5 us (10%)
    ppermute x4, starting transfers between devices, shifted(): return lax.ppermute(value, axis, pairs)  17.1 us
    unnamed x26, local copies, waits for them, and re-layouts  16.4 us
    dot_general x4, matrix products, one_block(): jnp.einsum('qk,kd->qd', weight_bf, value_block, preferred_element_type=jn...  15.7 us
    dot_general x4, matrix products, key_terms(): jnp.einsum('qk,qd->kd', weight_bf, grad_rows, preferred_element_type=jnp....  10.9 us
    dot_general x4, matrix products, one_block(): jnp.einsum('qd,kd->qk', query_rows, key_block, preferred_element_type=jnp...  9.35 us
    dot_general x4, matrix products, score_grads(): jnp.einsum('qd,kd->qk', grad_rows, value_block, preferred_element_type=jn...  9.2 us
    all_to_all x1, waiting for transfers between devices, shards(): lax.all_to_all(query_in, 'head', split_axis=1, concat_axis=0, tiled=True)  8.55 us
    all_to_all x1, waiting for transfers between devices, shards(): lax.all_to_all(key_in, 'head', split_axis=1, concat_axis=0, tiled=True)  8.54 us
  transfers between devices with their start and end apart: 12, of which 7 were waited for; matrix products, arithmetic and copies ran while one was open for 12% of the time, Pallas kernels for 0%

profile of v1, /device:TPU:225, one launch (start us, length us, event | category | flops | bytes accessed | tf_op | source)
XLA Modules:
  0.0 214.4 jit_solution(13711695960462773591)
XLA Ops:
  2.6 6.8 %all-to-all-start.1 = ((bf16[128,16,128]{2,0,1:T(8,128)(2,1)}), bf16[128,16,128]{2,0,1:T(8,128)(2,1)S(1)}, u32[]{:S(2)}, u32[]{:S(2)}) async-start(bf16[128,16,128]{2,0,1:T(8,128)(2,1)} %copy_bitcast_fusion.1), calls=%async_computation.1 | async-start | bytes 1048576 | tf_op jit(solution)/shard_map/all_to_all | solution.py:66
  11.3 8.5 %all-to-all-done.1 = bf16[128,16,128]{2,0,1:T(8,128)(2,1)S(1)} async-done(((bf16[128,16,128]{2,0,1:T(8,128)(2,1)}), bf16[128,16,128]{2,0,1:T(8,128)(2,1)S(1)}, u32[]{:S(2)}, u32[]{:S(2)}) %all-to-all-start.1) | async-done | bytes 524320 | tf_op jit(solution)/shard_map/all_to_all | solution.py:66
  19.9 3.6 %all-to-all-start.2 = ((bf16[128,16,128]{2,0,1:T(8,128)(2,1)}), bf16[128,16,128]{2,0,1:T(8,128)(2,1)S(1)}, u32[]{:S(2)}, u32[]{:S(2)}) async-start(bf16[128,16,128]{2,0,1:T(8,128)(2,1)} %copy_bitcast_fusion), calls=%async_computation.2 | async-start | bytes 1048576 | tf_op jit(solution)/shard_map/all_to_all | solution.py:67
  25.5 7.6 %all-to-all-done.2 = bf16[128,16,128]{2,0,1:T(8,128)(2,1)S(1)} async-done(((bf16[128,16,128]{2,0,1:T(8,128)(2,1)}), bf16[128,16,128]{2,0,1:T(8,128)(2,1)S(1)}, u32[]{:S(2)}, u32[]{:S(2)}) %all-to-all-start.2) | async-done | bytes 524320 | tf_op jit(solution)/shard_map/all_to_all | solution.py:67
  33.1 3.6 %all-to-all-start.3 = ((bf16[128,16,128]{0,2,1:T(8,128)(2,1)}), bf16[128,16,128]{0,2,1:T(8,128)(2,1)S(1)}, u32[]{:S(2)}, u32[]{:S(2)}) async-start(bf16[128,16,128]{0,2,1:T(8,128)(2,1)} %bitcast.18), calls=%async_computation.3 | async-start | bytes 1048576 | tf_op jit(solution)/shard_map/all_to_all | solution.py:68
  38.2 7.5 %collective-permute-start = (bf16[256,128]{1,0:T(8,128)(2,1)S(1)}, bf16[256,128]{1,0:T(8,128)(2,1)S(1)}, u32[]{:S(2)}, u32[]{:S(2)}) collective-permute-start(bf16[256,128]{1,0:T(8,128)(2,1)S(1)} %bitcast.150), channel_id=1, source_target_pairs={{0,16},{16,32},{32,48},{48,64},{64,80},{80,96},{96,112},{112,128},... | collective-permute-start | bytes 196616 | tf_op jit(solution)/shard_map/ppermute | solution.py:13
  47.7 6.9 %all-to-all-start = ((bf16[128,16,128]{2,0,1:T(8,128)(2,1)}), bf16[128,16,128]{2,0,1:T(8,128)(2,1)S(1)}, u32[]{:S(2)}, u32[]{:S(2)}) async-start(bf16[128,16,128]{2,0,1:T(8,128)(2,1)} %copy_bitcast_fusion.2), calls=%async_computation | async-start | bytes 1048576 | tf_op jit(solution)/shard_map/all_to_all | solution.py:65
  56.6 8.5 %all-to-all-done = bf16[128,16,128]{2,0,1:T(8,128)(2,1)S(1)} async-done(((bf16[128,16,128]{2,0,1:T(8,128)(2,1)}), bf16[128,16,128]{2,0,1:T(8,128)(2,1)S(1)}, u32[]{:S(2)}, u32[]{:S(2)}) %all-to-all-start) | async-done | bytes 524320 | tf_op jit(solution)/shard_map/all_to_all | solution.py:65
  65.1 79.0 %while.33 = (s32[]{:T(128)}, bf16[4,512,128]{2,1,0:T(8,128)(2,1)}, bf16[4,512,128]{2,1,0:T(8,128)(2,1)}, f32[4,2304,128]{2,1,0:T(8,128)}, f32[4,2304,128]{2,1,0:...) while((s32[]{:T(128)}, bf16[4,512,128]{2,1,0:T(8,128)(2,1)}, ...), condition=%wide.region_8.9_spmd, body=%wide.region_2.8_spmd.sunk | while | flops 1855588608 | bytes 75382872 | solution.py:106
  74.5 3.9 %multiply_reduce_fusion.2 = (f32[512]{0:T(512)S(1)}, bf16[512,128]{0,1:T(8,128)(2,1)S(1)}) fusion(bf16[1,512,128]{1,2,0:T(8,128)(2,1)S(1)} %copy.95, bf16[2304,128]{1,0:T(8,128)(2,1)S(1)} %copy-done.3, f32[512,2304]{1,0:T(8,128)} %copy-done.1, f32[512]{0:T(512)S(1)} %log_add_fusion.2, s32[512]{0:T(512)S(1)} %bitcast.147, ...), kind=kOutput, calls=%fused_computation.20.clone.1 | convolution fusion | flops 309394944 | bytes 5597184 | tf_op jit(solution)/shard_map/while/body/eval_jaxpr/while/body/eval_jaxpr/qk,kd->qd/dot_general | solution.py:51
  94.2 3.9 %multiply_reduce_fusion.2 = (f32[512]{0:T(512)S(1)}, bf16[512,128]{0,1:T(8,128)(2,1)S(1)}) fusion(bf16[1,512,128]{1,2,0:T(8,128)(2,1)S(1)} %copy.95, bf16[2304,128]{1,0:T(8,128)(2,1)S(1)} %copy-done.3, f32[512,2304]{1,0:T(8,128)} %copy-done.1, f32[512]{0:T(512)S(1)} %log_add_fusion.2, s32[512]{0:T(512)S(1)} %bitcast.147, ...), kind=kOutput, calls=%fused_computation.20.clone.1 | convolution fusion | flops 309394944 | bytes 5597184 | tf_op jit(solution)/shard_map/while/body/eval_jaxpr/while/body/eval_jaxpr/qk,kd->qd/dot_general | solution.py:51
  113.9 3.9 %multiply_reduce_fusion.2 = (f32[512]{0:T(512)S(1)}, bf16[512,128]{0,1:T(8,128)(2,1)S(1)}) fusion(bf16[1,512,128]{1,2,0:T(8,128)(2,1)S(1)} %copy.95, bf16[2304,128]{1,0:T(8,128)(2,1)S(1)} %copy-done.3, f32[512,2304]{1,0:T(8,128)} %copy-done.1, f32[512]{0:T(512)S(1)} %log_add_fusion.2, s32[512]{0:T(512)S(1)} %bitcast.147, ...), kind=kOutput, calls=%fused_computation.20.clone.1 | convolution fusion | flops 309394944 | bytes 5597184 | tf_op jit(solution)/shard_map/while/body/eval_jaxpr/while/body/eval_jaxpr/qk,kd->qd/dot_general | solution.py:51
  130.8 2.8 %fusion.56 = f32[4,2304,128]{2,1,0:T(8,128)} fusion(f32[4,2304,128]{2,1,0:T(8,128)} %get-tuple-element.443, s32[]{:T(128)} %get-tuple-element.439, bf16[1,512,128]{2,1,0:T(8,128)(2,1)S(1)} %constant_dynamic-slice_fusion.4, f32[512,2304]{1,0:T(8,128)S(1)} %get-tuple-element.421, f32[512]{0:T(512)S(1)} %log_add_fusion.2, ...), kind=kOutput, calls=%fused_computation.11.clone.1 | convolution fusion | flops 309067776 | bytes 6054400 | tf_op jit(solution)/shard_map/while/body/eval_jaxpr/while/body/eval_jaxpr/qk,qd->kd/dot_general | solution.py:37
  133.7 3.9 %multiply_reduce_fusion.2 = (f32[512]{0:T(512)S(1)}, bf16[512,128]{0,1:T(8,128)(2,1)S(1)}) fusion(bf16[1,512,128]{1,2,0:T(8,128)(2,1)S(1)} %copy.95, bf16[2304,128]{1,0:T(8,128)(2,1)S(1)} %copy-done.3, f32[512,2304]{1,0:T(8,128)} %copy-done.1, f32[512]{0:T(512)S(1)} %log_add_fusion.2, s32[512]{0:T(512)S(1)} %bitcast.147, ...), kind=kOutput, calls=%fused_computation.20.clone.1 | convolution fusion | flops 309394944 | bytes 5597184 | tf_op jit(solution)/shard_map/while/body/eval_jaxpr/while/body/eval_jaxpr/qk,kd->qd/dot_general | solution.py:51
  146.9 3.8 %collective-permute-start.2 = (f32[1,256,128]{2,1,0:T(8,128)S(1)}, f32[1,256,128]{2,1,0:T(8,128)S(1)}, u32[]{:S(2)}, u32[]{:S(2)}) collective-permute-start(f32[1,256,128]{2,1,0:T(8,128)S(1)} %slice.116), channel_id=1, source_target_pairs={{16,0},{32,16},{48,32},{64,48},{80,64},{96,80},{112,96},{128,112},... | collective-permute-start | bytes 393224 | tf_op jit(solution)/shard_map/ppermute | solution.py:13
  150.8 3.6 %all-to-all-start.4 = ((bf16[16,128,128]{2,1,0:T(8,128)(2,1)}), bf16[16,128,128]{2,1,0:T(8,128)(2,1)S(1)}, u32[]{:S(2)}, u32[]{:S(2)}) async-start(bf16[16,128,128]{2,1,0:T(8,128)(2,1)} %bitcast.21), calls=%async_computation.4 | async-start | bytes 1048576 | tf_op jit(solution)/shard_map/all_to_all | solution.py:122
  162.5 3.3 %all-to-all-done.4 = bf16[16,128,128]{2,1,0:T(8,128)(2,1)S(1)} async-done(((bf16[16,128,128]{2,1,0:T(8,128)(2,1)}), bf16[16,128,128]{2,1,0:T(8,128)(2,1)S(1)}, u32[]{:S(2)}, u32[]{:S(2)}) %all-to-all-start.4) | async-done | bytes 524320 | tf_op jit(solution)/shard_map/all_to_all | solution.py:122
  165.7 3.8 %all-to-all-start.5 = ((bf16[16,128,128]{2,1,0:T(8,128)(2,1)}), bf16[16,128,128]{2,1,0:T(8,128)(2,1)S(1)}, u32[]{:S(2)}, u32[]{:S(2)}) async-start(bf16[16,128,128]{2,1,0:T(8,128)(2,1)} %bitcast.149), calls=%async_computation.5 | async-start | bytes 1048576 | tf_op jit(solution)/shard_map/all_to_all | solution.py:130
  171.4 8.4 %all-to-all-done.5 = bf16[16,128,128]{2,1,0:T(8,128)(2,1)S(1)} async-done(((bf16[16,128,128]{2,1,0:T(8,128)(2,1)}), bf16[16,128,128]{2,1,0:T(8,128)(2,1)S(1)}, u32[]{:S(2)}, u32[]{:S(2)}) %all-to-all-start.5) | async-done | bytes 524320 | tf_op jit(solution)/shard_map/all_to_all | solution.py:130
  179.8 3.6 %all-to-all-start.6 = ((bf16[16,128,128]{2,1,0:T(8,128)(2,1)}), bf16[16,128,128]{2,1,0:T(8,128)(2,1)S(1)}, u32[]{:S(2)}, u32[]{:S(2)}) async-start(bf16[16,128,128]{2,1,0:T(8,128)(2,1)} %constant_dynamic-update-slice_fusion.1), calls=%async_computation.6 | async-start | bytes 1048576 | tf_op jit(solution)/shard_map/all_to_all | solution.py:132
  186.1 3.9 %collective-permute-start.3 = (f32[1,256,128]{2,1,0:T(8,128)S(1)}, f32[1,256,128]{2,1,0:T(8,128)S(1)}, u32[]{:S(2)}, u32[]{:S(2)}) collective-permute-start(f32[1,256,128]{2,1,0:T(8,128)S(1)} %slice.119), channel_id=1, source_target_pairs={{16,0},{32,16},{48,32},{64,48},{80,64},{96,80},{112,96},{128,112},... | collective-permute-start | bytes 393224 | tf_op jit(solution)/shard_map/ppermute | solution.py:13
  190.9 3.1 %collective-permute-done.3 = f32[1,256,128]{2,1,0:T(8,128)S(1)} collective-permute-done((f32[1,256,128]{2,1,0:T(8,128)S(1)}, f32[1,256,128]{2,1,0:T(8,128)S(1)}, u32[]{:S(2)}, u32[]{:S(2)}) %collective-permute-start.3) | collective-permute-done | bytes 131104 | tf_op jit(solution)/shard_map/ppermute | solution.py:13
  194.6 6.3 %all-to-all-start.7 = ((bf16[16,128,128]{2,1,0:T(8,128)(2,1)}), bf16[16,128,128]{2,1,0:T(8,128)(2,1)S(1)}, u32[]{:S(2)}, u32[]{:S(2)}) async-start(bf16[16,128,128]{2,1,0:T(8,128)(2,1)} %bitcast.31), calls=%async_computation.7 | async-start | bytes 1048576 | tf_op jit(solution)/shard_map/all_to_all | solution.py:137
  204.8 8.4 %all-to-all-done.7 = bf16[16,128,128]{2,1,0:T(8,128)(2,1)S(1)} async-done(((bf16[16,128,128]{2,1,0:T(8,128)(2,1)}), bf16[16,128,128]{2,1,0:T(8,128)(2,1)S(1)}, u32[]{:S(2)}, u32[]{:S(2)}) %all-to-all-start.7) | async-done | bytes 524320 | tf_op jit(solution)/shard_map/all_to_all | solution.py:137
  (212 shorter events, 93.3 us)
Async XLA Ops:
  0.6 36.1 %copy-start.7 = (s32[512]{0:T(512)S(1)}, s32[512]{0:T(512)}, u32[]{:S(2)}) copy-start(s32[512]{0:T(512)} %param.15) | copy-start | bytes 6148
  1.7 35.6 %copy-start.4 = (bf16[128,2048]{1,0:T(8,128)(2,1)S(1)}, bf16[128,2048]{1,0:T(8,128)(2,1)}, u32[]{:S(2)}) copy-start(bf16[128,2048]{1,0:T(8,128)(2,1)} %param.11) | copy-start | bytes 1572868
  2.6 17.3 %all-to-all-start.1 = ((bf16[128,16,128]{2,0,1:T(8,128)(2,1)}), bf16[128,16,128]{2,0,1:T(8,128)(2,1)S(1)}, u32[]{:S(2)}, u32[]{:S(2)}) async-start(bf16[128,16,128]{2,0,1:T(8,128)(2,1)} %copy_bitcast_fusion.1), calls=%async_computation.1 | async-start | bytes 1048576 | tf_op jit(solution)/shard_map/all_to_all | solution.py:66
  19.9 13.2 %all-to-all-start.2 = ((bf16[128,16,128]{2,0,1:T(8,128)(2,1)}), bf16[128,16,128]{2,0,1:T(8,128)(2,1)S(1)}, u32[]{:S(2)}, u32[]{:S(2)}) async-start(bf16[128,16,128]{2,0,1:T(8,128)(2,1)} %copy_bitcast_fusion), calls=%async_computation.2 | async-start | bytes 1048576 | tf_op jit(solution)/shard_map/all_to_all | solution.py:67
  33.1 14.5 %all-to-all-start.3 = ((bf16[128,16,128]{0,2,1:T(8,128)(2,1)}), bf16[128,16,128]{0,2,1:T(8,128)(2,1)S(1)}, u32[]{:S(2)}, u32[]{:S(2)}) async-start(bf16[128,16,128]{0,2,1:T(8,128)(2,1)} %bitcast.18), calls=%async_computation.3 | async-start | bytes 1048576 | tf_op jit(solution)/shard_map/all_to_all | solution.py:68
  38.2 16.6 %collective-permute-start = (bf16[256,128]{1,0:T(8,128)(2,1)S(1)}, bf16[256,128]{1,0:T(8,128)(2,1)S(1)}, u32[]{:S(2)}, u32[]{:S(2)}) collective-permute-start(bf16[256,128]{1,0:T(8,128)(2,1)S(1)} %bitcast.150), channel_id=1, source_target_pairs={{0,16},{16,32},{32,48},{48,64},{64,80},{80,96},{96,112},{112,128},... | collective-permute-start | bytes 196616 | tf_op jit(solution)/shard_map/ppermute | solution.py:13
  45.7 10.0 %collective-permute-start.1 = (bf16[256,128]{1,0:T(8,128)(2,1)S(1)}, bf16[256,128]{1,0:T(8,128)(2,1)S(1)}, u32[]{:S(2)}, u32[]{:S(2)}) collective-permute-start(bf16[256,128]{1,0:T(8,128)(2,1)S(1)} %bitcast.151), channel_id=1, source_target_pairs={{0,16},{16,32},{32,48},{48,64},{64,80},{80,96},{96,112},{112,128},... | collective-permute-start | bytes 196616 | tf_op jit(solution)/shard_map/ppermute | solution.py:13
  47.7 17.5 %all-to-all-start = ((bf16[128,16,128]{2,0,1:T(8,128)(2,1)}), bf16[128,16,128]{2,0,1:T(8,128)(2,1)S(1)}, u32[]{:S(2)}, u32[]{:S(2)}) async-start(bf16[128,16,128]{2,0,1:T(8,128)(2,1)} %copy_bitcast_fusion.2), calls=%async_computation | async-start | bytes 1048576 | tf_op jit(solution)/shard_map/all_to_all | solution.py:65
  65.1 6.0 %copy-start.5 = (s32[4,512]{1,0:T(4,128)}, s32[4,512]{1,0:T(4,128)S(1)}, u32[]{:S(2)}) copy-start(s32[4,512]{1,0:T(4,128)S(1)} %get-tuple-element.458) | copy-start | bytes 24580 | tf_op jit(solution)/shard_map/while/body/eval_jaxpr/while
  65.1 6.0 %copy-start.8 = (s32[5,1]{0,1:T(1,128)}, s32[5,1]{0,1:T(1,128)S(1)}, u32[]{:S(2)}) copy-start(s32[5,1]{0,1:T(1,128)S(1)} %get-tuple-element.459) | copy-start | bytes 64 | tf_op jit(solution)/shard_map/while/body/eval_jaxpr/while
  84.9 6.0 %copy-start.5 = (s32[4,512]{1,0:T(4,128)}, s32[4,512]{1,0:T(4,128)S(1)}, u32[]{:S(2)}) copy-start(s32[4,512]{1,0:T(4,128)S(1)} %get-tuple-element.458) | copy-start | bytes 24580 | tf_op jit(solution)/shard_map/while/body/eval_jaxpr/while
  84.9 6.0 %copy-start.8 = (s32[5,1]{0,1:T(1,128)}, s32[5,1]{0,1:T(1,128)S(1)}, u32[]{:S(2)}) copy-start(s32[5,1]{0,1:T(1,128)S(1)} %get-tuple-element.459) | copy-start | bytes 64 | tf_op jit(solution)/shard_map/while/body/eval_jaxpr/while
  100.5 4.1 %copy-start.6 = (s32[4,512]{1,0:T(4,128)S(1)}, s32[4,512]{1,0:T(4,128)}, u32[]{:S(2)}) copy-start(s32[4,512]{1,0:T(4,128)} %copy-done.5) | copy-start | bytes 24580 | tf_op jit(solution)/shard_map/while/body/eval_jaxpr/while
  104.6 6.0 %copy-start.5 = (s32[4,512]{1,0:T(4,128)}, s32[4,512]{1,0:T(4,128)S(1)}, u32[]{:S(2)}) copy-start(s32[4,512]{1,0:T(4,128)S(1)} %get-tuple-element.458) | copy-start | bytes 24580 | tf_op jit(solution)/shard_map/while/body/eval_jaxpr/while
  104.6 6.0 %copy-start.8 = (s32[5,1]{0,1:T(1,128)}, s32[5,1]{0,1:T(1,128)S(1)}, u32[]{:S(2)}) copy-start(s32[5,1]{0,1:T(1,128)S(1)} %get-tuple-element.459) | copy-start | bytes 64 | tf_op jit(solution)/shard_map/while/body/eval_jaxpr/while
  120.2 4.1 %copy-start.6 = (s32[4,512]{1,0:T(4,128)S(1)}, s32[4,512]{1,0:T(4,128)}, u32[]{:S(2)}) copy-start(s32[4,512]{1,0:T(4,128)} %copy-done.5) | copy-start | bytes 24580 | tf_op jit(solution)/shard_map/while/body/eval_jaxpr/while
  124.3 6.0 %copy-start.5 = (s32[4,512]{1,0:T(4,128)}, s32[4,512]{1,0:T(4,128)S(1)}, u32[]{:S(2)}) copy-start(s32[4,512]{1,0:T(4,128)S(1)} %get-tuple-element.458) | copy-start | bytes 24580 | tf_op jit(solution)/shard_map/while/body/eval_jaxpr/while
  124.3 6.0 %copy-start.8 = (s32[5,1]{0,1:T(1,128)}, s32[5,1]{0,1:T(1,128)S(1)}, u32[]{:S(2)}) copy-start(s32[5,1]{0,1:T(1,128)S(1)} %get-tuple-element.459) | copy-start | bytes 64 | tf_op jit(solution)/shard_map/while/body/eval_jaxpr/while
  146.9 7.5 %collective-permute-start.2 = (f32[1,256,128]{2,1,0:T(8,128)S(1)}, f32[1,256,128]{2,1,0:T(8,128)S(1)}, u32[]{:S(2)}, u32[]{:S(2)}) collective-permute-start(f32[1,256,128]{2,1,0:T(8,128)S(1)} %slice.116), channel_id=1, source_target_pairs={{16,0},{32,16},{48,32},{64,48},{80,64},{96,80},{112,96},{128,112},... | collective-permute-start | bytes 393224 | tf_op jit(solution)/shard_map/ppermute | solution.py:13
  150.8 15.0 %all-to-all-start.4 = ((bf16[16,128,128]{2,1,0:T(8,128)(2,1)}), bf16[16,128,128]{2,1,0:T(8,128)(2,1)S(1)}, u32[]{:S(2)}, u32[]{:S(2)}) async-start(bf16[16,128,128]{2,1,0:T(8,128)(2,1)} %bitcast.21), calls=%async_computation.4 | async-start | bytes 1048576 | tf_op jit(solution)/shard_map/all_to_all | solution.py:122
  165.7 14.1 %all-to-all-start.5 = ((bf16[16,128,128]{2,1,0:T(8,128)(2,1)}), bf16[16,128,128]{2,1,0:T(8,128)(2,1)S(1)}, u32[]{:S(2)}, u32[]{:S(2)}) async-start(bf16[16,128,128]{2,1,0:T(8,128)(2,1)} %bitcast.149), calls=%async_computation.5 | async-start | bytes 1048576 | tf_op jit(solution)/shard_map/all_to_all | solution.py:130
  179.8 14.8 %all-to-all-start.6 = ((bf16[16,128,128]{2,1,0:T(8,128)(2,1)}), bf16[16,128,128]{2,1,0:T(8,128)(2,1)S(1)}, u32[]{:S(2)}, u32[]{:S(2)}) async-start(bf16[16,128,128]{2,1,0:T(8,128)(2,1)} %constant_dynamic-update-slice_fusion.1), calls=%async_computation.6 | async-start | bytes 1048576 | tf_op jit(solution)/shard_map/all_to_all | solution.py:132
  186.1 7.8 %collective-permute-start.3 = (f32[1,256,128]{2,1,0:T(8,128)S(1)}, f32[1,256,128]{2,1,0:T(8,128)S(1)}, u32[]{:S(2)}, u32[]{:S(2)}) collective-permute-start(f32[1,256,128]{2,1,0:T(8,128)S(1)} %slice.119), channel_id=1, source_target_pairs={{16,0},{32,16},{48,32},{64,48},{80,64},{96,80},{112,96},{128,112},... | collective-permute-start | bytes 393224 | tf_op jit(solution)/shard_map/ppermute | solution.py:13
  194.6 18.6 %all-to-all-start.7 = ((bf16[16,128,128]{2,1,0:T(8,128)(2,1)}), bf16[16,128,128]{2,1,0:T(8,128)(2,1)S(1)}, u32[]{:S(2)}, u32[]{:S(2)}) async-start(bf16[16,128,128]{2,1,0:T(8,128)(2,1)} %bitcast.31), calls=%async_computation.7 | async-start | bytes 1048576 | tf_op jit(solution)/shard_map/all_to_all | solution.py:137
  (27 other events, 85.4 us)
